TPU v7x, 32 devices: a whole 2x2x4 slice. The times are simulated.
32 devices in a mesh: groups: 2 (over x), ctx: 16 (over z, y, core).
Axes of the slice: x: 2, y: 2, z: 4, core: 2. Of those that a mesh axis runs over, the one named last changes fastest.
Arguments:
- receptance: bfloat16 [4096, 2048], P(('groups', 'ctx')), parts along dimension 0, may hold values from -6 to 6
- decay_logit: bfloat16 [4096, 2048], P(('groups', 'ctx')), parts along dimension 0, may hold values from -16 to 2
- token_keys: bfloat16 [4096, 2048], P(('groups', 'ctx')), parts along dimension 0, may hold values from -6 to 6
- token_values: bfloat16 [4096, 2048], P(('groups', 'ctx')), parts along dimension 0, may hold values from -6 to 6
- removal_key: bfloat16 [4096, 2048], P(('groups', 'ctx')), parts along dimension 0, may hold values from -6 to 6
- removal_rate: bfloat16 [4096, 2048], P(('groups', 'ctx')), parts along dimension 0, may hold values from 0 to 1
- output_grad: bfloat16 [4096, 2048], P(('groups', 'ctx')), parts along dimension 0, may hold values from -0.0390625 to 0.0390625
Outputs:
- grad_receptance: bfloat16 [4096, 2048], P(('groups', 'ctx')), parts along dimension 0
- grad_decay: bfloat16 [4096, 2048], P(('groups', 'ctx')), parts along dimension 0
- grad_keys: bfloat16 [4096, 2048], P(('groups', 'ctx')), parts along dimension 0
- grad_values: bfloat16 [4096, 2048], P(('groups', 'ctx')), parts along dimension 0
- grad_removal_key: bfloat16 [4096, 2048], P(('groups', 'ctx')), parts along dimension 0
- grad_removal_rate: bfloat16 [4096, 2048], P(('groups', 'ctx')), parts along dimension 0
There are 2 independent parts, one for each index of `groups`. A program takes and returns all parts, laid end to end along the dimension named above; each array names one. Nothing has to cross between parts.
All inputs are finite; a program needn't handle non-finite values.
Results may differ from a plain program's by a relative error of at most 0.001.
Values sent between devices are 32-bit elements; how exact they have to be, the bound alone decides.
A program may use at most 448 MiB of HBM per device.

v0:
```python
import jax
import jax.numpy as jnp
from jax import lax
from jax.sharding import PartitionSpec as P

HEADS = 32
HS = 64
BLOCK = 128


DECAY_SCALE = 0.6065306597126334
precise = lax.Precision.HIGHEST


def entering(part, axis, combine, identity):
    count = lax.axis_size(axis)
    place = lax.axis_index(axis)
    ahead = count - 1 - place
    gathered = jax.tree.map(lambda a: lax.all_gather(a, axis), part)
    state = jax.tree.map(lambda a, e: jnp.zeros_like(a) + jnp.asarray(e, a.dtype), part, identity)

    def one(hop, state):
        source = count - 1 - hop
        return combine(
            state, jax.tree.map(lambda a: lax.dynamic_index_in_dim(a, source, 0, False), gathered)
        )

    return lax.fori_loop(0, ahead, one, state)


def shifted(x, axis, by):
    size = lax.axis_size(axis)
    pairs = [(i, i + by) for i in range(size) if 0 <= i + by < size]
    return lax.ppermute(x, axis, pairs)


def prepare(receptance, decay_logit, token_keys, token_values, removal_key, removal_rate):

    def headed(array):
        return array.astype(jnp.float32).reshape(array.shape[0], HEADS, HS)

    queries = headed(receptance)
    log_decay = -DECAY_SCALE * jax.nn.sigmoid(headed(decay_logit))
    direction = headed(removal_key)
    direction = direction * lax.rsqrt(
        jnp.sum(direction * direction, axis=-1, keepdims=True) + 1e-06
    )
    return (
        queries,
        log_decay,
        headed(token_keys),
        headed(token_values),
        -direction,
        direction * headed(removal_rate),
    )


def to_blocks(array):
    count = array.shape[0] // BLOCK
    return array.reshape(count, BLOCK, array.shape[1], array.shape[2]).transpose(0, 2, 1, 3)


def unit_lower_inverse(lower):
    width = lower.shape[-1]
    result = jnp.eye(width, dtype=jnp.float32) + lower
    power = lower
    reach = 2
    while reach < width:
        power = jnp.einsum("hts,hsu->htu", power, power, precision=precise)
        result = result + jnp.einsum("hts,hsu->htu", result, power, precision=precise)
        reach = reach * 2
    return result


def block_step(state, pieces):
    queries, log_decay, key_rows, value_rows, take_dir, give_dir = pieces
    cumulative = jnp.cumsum(log_decay, axis=1)
    previous = cumulative - log_decay
    take_scaled = take_dir * jnp.exp(previous)
    query_scaled = queries * jnp.exp(cumulative)
    give_scaled = give_dir * jnp.exp(-cumulative)
    key_scaled = key_rows * jnp.exp(-cumulative)
    strict = jnp.tril(jnp.ones((BLOCK, BLOCK), jnp.float32), -1)
    inclusive = jnp.tril(jnp.ones((BLOCK, BLOCK), jnp.float32))
    take_give = jnp.einsum("htj,hsj->hts", take_scaled, give_scaled, precision=precise) * strict
    take_key = jnp.einsum("htj,hsj->hts", take_scaled, key_scaled, precision=precise) * strict
    right_side = jnp.einsum("htj,hij->hti", take_scaled, state, precision=precise) + jnp.einsum(
        "hts,hsi->hti", take_key, value_rows, precision=precise
    )
    inverse = unit_lower_inverse(take_give)
    removed = jnp.einsum("hts,hsi->hti", inverse, right_side, precision=precise)
    query_give = (
        jnp.einsum("htj,hsj->hts", query_scaled, give_scaled, precision=precise) * inclusive
    )
    query_key = jnp.einsum("htj,hsj->hts", query_scaled, key_scaled, precision=precise) * inclusive
    outputs = jnp.einsum("htj,hij->hti", query_scaled, state, precision=precise)
    outputs = outputs + jnp.einsum("hts,hsi->hti", query_give, removed, precision=precise)
    outputs = outputs + jnp.einsum("hts,hsi->hti", query_key, value_rows, precision=precise)
    final_decay = jnp.exp(cumulative[:, -1:, :])
    state = state * final_decay
    state = state + jnp.einsum(
        "hsi,hsj->hij", removed, give_scaled * final_decay, precision=precise
    )
    state = state + jnp.einsum(
        "hsi,hsj->hij", value_rows, key_scaled * final_decay, precision=precise
    )
    return (state, outputs)


def local_pass(start, queries, log_decay, key_rows, value_rows, take_dir, give_dir):
    pieces = tuple(
        (
            to_blocks(array)
            for array in (queries, log_decay, key_rows, value_rows, take_dir, give_dir)
        )
    )
    final, outputs = lax.scan(block_step, start, pieces)
    rows = queries.shape[0]
    outputs = outputs.transpose(0, 2, 1, 3).reshape(rows, outputs.shape[1], outputs.shape[3])
    return (outputs, final)


def full_layer(receptance, decay_logit, token_keys, token_values, removal_key, removal_rate, start):
    queries, log_decay, key_rows, value_rows, take_dir, give_dir = prepare(
        receptance, decay_logit, token_keys, token_values, removal_key, removal_rate
    )
    return local_pass(start, queries, log_decay, key_rows, value_rows, take_dir, give_dir)


def compose(left, right):
    return jnp.einsum("hij,hjk->hik", left, right, precision=precise)


def adjoint_combine(earlier, later):
    return (compose(earlier[0], later[0]), later[1] + compose(earlier[1], later[0]))


def per_device(
    receptance, decay_logit, token_keys, token_values, removal_key, removal_rate, output_grad
):
    queries, log_decay, key_rows, value_rows, take_dir, give_dir = prepare(
        receptance, decay_logit, token_keys, token_values, removal_key, removal_rate
    )
    rows = receptance.shape[0]
    grad_rows = output_grad.astype(jnp.float32).reshape(rows, HEADS, HS)
    identity = jnp.broadcast_to(jnp.eye(HS, dtype=jnp.float32), (HEADS, HS, HS))
    zero_state = jnp.zeros((HEADS, HS, HS), jnp.float32)
    stacked_start = jnp.concatenate([identity, zero_state], axis=1)
    stacked_values = jnp.concatenate([jnp.zeros_like(value_rows), value_rows], axis=2)
    unused, stacked_end = local_pass(
        stacked_start, queries, log_decay, key_rows, stacked_values, take_dir, give_dir
    )
    transfer = stacked_end[:, :HS, :]
    local_end = stacked_end[:, HS:, :]

    def start_outputs(start):
        return local_pass(start, queries, log_decay, key_rows, value_rows, take_dir, give_dir)[0]

    ignored, start_pullback = jax.vjp(start_outputs, zero_state)
    local_adjoint = start_pullback(grad_rows)[0]
    transposed = jnp.swapaxes(transfer, 1, 2)
    product_after, adjoint_end = entering(
        (transposed, local_adjoint), "ctx", adjoint_combine, (identity, zero_state)
    )

    def advance(step, current):
        return shifted(compose(current, transfer) + local_end, "ctx", 1)

    start = lax.fori_loop(0, lax.axis_size("ctx") - 1, advance, zero_state)
    primal, pullback = jax.vjp(
        full_layer,
        receptance,
        decay_logit,
        token_keys,
        token_values,
        removal_key,
        removal_rate,
        start,
    )
    grads = pullback((grad_rows, adjoint_end))
    return (grads[0], grads[1], grads[2], grads[3], grads[4], grads[5])


def solution(mesh):
    placed = (
        P(("groups", "ctx"), None),
        P(("groups", "ctx"), None),
        P(("groups", "ctx"), None),
        P(("groups", "ctx"), None),
        P(("groups", "ctx"), None),
        P(("groups", "ctx"), None),
        P(("groups", "ctx"), None),
    )
    return jax.shard_map(
        per_device,
        mesh=mesh,
        in_specs=placed,
        out_specs=(
            P(("groups", "ctx"), None),
            P(("groups", "ctx"), None),
            P(("groups", "ctx"), None),
            P(("groups", "ctx"), None),
            P(("groups", "ctx"), None),
            P(("groups", "ctx"), None),
        ),
        check_vma=False,
    )
```

profile of v0, /device:TPU:0, one launch (start us, length us, event | category | flops | bytes accessed | tf_op | source)
XLA Modules:
  0.0 1077.7 jit_solution(15304416542396342112)
XLA Ops:
  32.3 7.5 multiply_bitcast_fusion.2
  42.6 6.0 broadcast_multiply_fusion
  63.8 6.1 fusion.135
  102.9 7.0 fusion.40
  130.2 8.2 fusion.27
  192.4 409.7 %while.19 = (s32[]{:T(128)}, f32[32,64,64]{2,1,0:T(8,128)S(1)}, f32[32,64,64]{2,1,0:T(8,128)}, f32[32,64,64]{2,1,0:T(8,128)}, s32[]{:T(128)}) while((s32[]{:T(128)}, f32[32,64,64]{2,1,0:T(8,128)S(1)}, f32[32,64,64]{2,1,0:T(8,128)}, f32[32,64,64]{2,1,0:T(8,128)}, s32[]{:T(128)}) %tuple.116), condition=%wide.region_3.4_spmd, body=%wide.region_2.3_spmd.sunk | while | flops 100794368 | bytes 4194405 | solution.py:169
  204.5 30.6 %collective-permute-start = (f32[32,64,64]{2,1,0:T(8,128)}, f32[32,64,64]{2,1,0:T(8,128)S(1)}, u32[]{:S(2)}, u32[]{:S(2)}) collective-permute-start(f32[32,64,64]{2,1,0:T(8,128)} %convolution_add_fusion.16), channel_id=1, source_target_pairs={{0,1},{1,2},{2,3},{3,4},{4,5},{5,6},{6,7},{7,8},{8,9},{9,10},{10,1... | collective-permute-start | bytes 1572872 | tf_op jit(solution)/shard_map/while/body/eval_jaxpr/ppermute | solution.py:34
  241.2 33.5 %collective-permute-start = (f32[32,64,64]{2,1,0:T(8,128)}, f32[32,64,64]{2,1,0:T(8,128)S(1)}, u32[]{:S(2)}, u32[]{:S(2)}) collective-permute-start(f32[32,64,64]{2,1,0:T(8,128)} %convolution_add_fusion.16), channel_id=1, source_target_pairs={{0,1},{1,2},{2,3},{3,4},{4,5},{5,6},{6,7},{7,8},{8,9},{9,10},{10,1... | collective-permute-start | bytes 1572872 | tf_op jit(solution)/shard_map/while/body/eval_jaxpr/ppermute | solution.py:34
  280.8 14.1 %collective-permute-start = (f32[32,64,64]{2,1,0:T(8,128)}, f32[32,64,64]{2,1,0:T(8,128)S(1)}, u32[]{:S(2)}, u32[]{:S(2)}) collective-permute-start(f32[32,64,64]{2,1,0:T(8,128)} %convolution_add_fusion.16), channel_id=1, source_target_pairs={{0,1},{1,2},{2,3},{3,4},{4,5},{5,6},{6,7},{7,8},{8,9},{9,10},{10,1... | collective-permute-start | bytes 1572872 | tf_op jit(solution)/shard_map/while/body/eval_jaxpr/ppermute | solution.py:34
  300.9 14.1 %collective-permute-start = (f32[32,64,64]{2,1,0:T(8,128)}, f32[32,64,64]{2,1,0:T(8,128)S(1)}, u32[]{:S(2)}, u32[]{:S(2)}) collective-permute-start(f32[32,64,64]{2,1,0:T(8,128)} %convolution_add_fusion.16), channel_id=1, source_target_pairs={{0,1},{1,2},{2,3},{3,4},{4,5},{5,6},{6,7},{7,8},{8,9},{9,10},{10,1... | collective-permute-start | bytes 1572872 | tf_op jit(solution)/shard_map/while/body/eval_jaxpr/ppermute | solution.py:34
  321.1 19.9 %collective-permute-start = (f32[32,64,64]{2,1,0:T(8,128)}, f32[32,64,64]{2,1,0:T(8,128)S(1)}, u32[]{:S(2)}, u32[]{:S(2)}) collective-permute-start(f32[32,64,64]{2,1,0:T(8,128)} %convolution_add_fusion.16), channel_id=1, source_target_pairs={{0,1},{1,2},{2,3},{3,4},{4,5},{5,6},{6,7},{7,8},{8,9},{9,10},{10,1... | collective-permute-start | bytes 1572872 | tf_op jit(solution)/shard_map/while/body/eval_jaxpr/ppermute | solution.py:34
  347.0 46.0 %collective-permute-start = (f32[32,64,64]{2,1,0:T(8,128)}, f32[32,64,64]{2,1,0:T(8,128)S(1)}, u32[]{:S(2)}, u32[]{:S(2)}) collective-permute-start(f32[32,64,64]{2,1,0:T(8,128)} %convolution_add_fusion.16), channel_id=1, source_target_pairs={{0,1},{1,2},{2,3},{3,4},{4,5},{5,6},{6,7},{7,8},{8,9},{9,10},{10,1... | collective-permute-start | bytes 1572872 | tf_op jit(solution)/shard_map/while/body/eval_jaxpr/ppermute | solution.py:34
  399.2 35.4 %collective-permute-start = (f32[32,64,64]{2,1,0:T(8,128)}, f32[32,64,64]{2,1,0:T(8,128)S(1)}, u32[]{:S(2)}, u32[]{:S(2)}) collective-permute-start(f32[32,64,64]{2,1,0:T(8,128)} %convolution_add_fusion.16), channel_id=1, source_target_pairs={{0,1},{1,2},{2,3},{3,4},{4,5},{5,6},{6,7},{7,8},{8,9},{9,10},{10,1... | collective-permute-start | bytes 1572872 | tf_op jit(solution)/shard_map/while/body/eval_jaxpr/ppermute | solution.py:34
  440.6 14.5 %collective-permute-start = (f32[32,64,64]{2,1,0:T(8,128)}, f32[32,64,64]{2,1,0:T(8,128)S(1)}, u32[]{:S(2)}, u32[]{:S(2)}) collective-permute-start(f32[32,64,64]{2,1,0:T(8,128)} %convolution_add_fusion.16), channel_id=1, source_target_pairs={{0,1},{1,2},{2,3},{3,4},{4,5},{5,6},{6,7},{7,8},{8,9},{9,10},{10,1... | collective-permute-start | bytes 1572872 | tf_op jit(solution)/shard_map/while/body/eval_jaxpr/ppermute | solution.py:34
  461.2 33.9 %collective-permute-start = (f32[32,64,64]{2,1,0:T(8,128)}, f32[32,64,64]{2,1,0:T(8,128)S(1)}, u32[]{:S(2)}, u32[]{:S(2)}) collective-permute-start(f32[32,64,64]{2,1,0:T(8,128)} %convolution_add_fusion.16), channel_id=1, source_target_pairs={{0,1},{1,2},{2,3},{3,4},{4,5},{5,6},{6,7},{7,8},{8,9},{9,10},{10,1... | collective-permute-start | bytes 1572872 | tf_op jit(solution)/shard_map/while/body/eval_jaxpr/ppermute | solution.py:34
  501.2 14.8 %collective-permute-start = (f32[32,64,64]{2,1,0:T(8,128)}, f32[32,64,64]{2,1,0:T(8,128)S(1)}, u32[]{:S(2)}, u32[]{:S(2)}) collective-permute-start(f32[32,64,64]{2,1,0:T(8,128)} %convolution_add_fusion.16), channel_id=1, source_target_pairs={{0,1},{1,2},{2,3},{3,4},{4,5},{5,6},{6,7},{7,8},{8,9},{9,10},{10,1... | collective-permute-start | bytes 1572872 | tf_op jit(solution)/shard_map/while/body/eval_jaxpr/ppermute | solution.py:34
  522.1 14.8 %collective-permute-start = (f32[32,64,64]{2,1,0:T(8,128)}, f32[32,64,64]{2,1,0:T(8,128)S(1)}, u32[]{:S(2)}, u32[]{:S(2)}) collective-permute-start(f32[32,64,64]{2,1,0:T(8,128)} %convolution_add_fusion.16), channel_id=1, source_target_pairs={{0,1},{1,2},{2,3},{3,4},{4,5},{5,6},{6,7},{7,8},{8,9},{9,10},{10,1... | collective-permute-start | bytes 1572872 | tf_op jit(solution)/shard_map/while/body/eval_jaxpr/ppermute | solution.py:34
  543.0 14.8 %collective-permute-start = (f32[32,64,64]{2,1,0:T(8,128)}, f32[32,64,64]{2,1,0:T(8,128)S(1)}, u32[]{:S(2)}, u32[]{:S(2)}) collective-permute-start(f32[32,64,64]{2,1,0:T(8,128)} %convolution_add_fusion.16), channel_id=1, source_target_pairs={{0,1},{1,2},{2,3},{3,4},{4,5},{5,6},{6,7},{7,8},{8,9},{9,10},{10,1... | collective-permute-start | bytes 1572872 | tf_op jit(solution)/shard_map/while/body/eval_jaxpr/ppermute | solution.py:34
  563.9 14.8 %collective-permute-start = (f32[32,64,64]{2,1,0:T(8,128)}, f32[32,64,64]{2,1,0:T(8,128)S(1)}, u32[]{:S(2)}, u32[]{:S(2)}) collective-permute-start(f32[32,64,64]{2,1,0:T(8,128)} %convolution_add_fusion.16), channel_id=1, source_target_pairs={{0,1},{1,2},{2,3},{3,4},{4,5},{5,6},{6,7},{7,8},{8,9},{9,10},{10,1... | collective-permute-start | bytes 1572872 | tf_op jit(solution)/shard_map/while/body/eval_jaxpr/ppermute | solution.py:34
  584.8 14.8 %collective-permute-start = (f32[32,64,64]{2,1,0:T(8,128)}, f32[32,64,64]{2,1,0:T(8,128)S(1)}, u32[]{:S(2)}, u32[]{:S(2)}) collective-permute-start(f32[32,64,64]{2,1,0:T(8,128)} %convolution_add_fusion.16), channel_id=1, source_target_pairs={{0,1},{1,2},{2,3},{3,4},{4,5},{5,6},{6,7},{7,8},{8,9},{9,10},{10,1... | collective-permute-start | bytes 1572872 | tf_op jit(solution)/shard_map/while/body/eval_jaxpr/ppermute | solution.py:34
  638.5 6.0 fusion.164
  644.6 139.0 %while.20 = (s32[]{:T(128)}, f32[32,64,64]{1,2,0:T(8,128)S(1)}, s32[]{:T(128)}, f32[16,32,64,64]{3,2,1,0:T(8,128)}, f32[16,32,64,64]{3,2,1,0:T(8,128)}, /*index=5*/s32[]{:T(128)}, s32[]{:T(128)}, s32[]{:T(128)}, s32[]{:T(128)}) while((s32[]{:T(128)}, f32[32,64,64]{1,2,0:T(8,128)S(1)}, s32[]{:T(128)}, f32[16,32,64,64]{3,2,1,0:T(8,128)}, ...), condition=%wide.region_5.6_spmd, body=%wide.region_4.5_spmd.sunk | while | flops 100794376 | bytes 7864495 | solution.py:28
  888.6 5.9 fusion.159
  917.8 8.9 fusion.95
  930.3 7.1 fusion.50
  937.5 6.7 add_multiply_fusion
  947.1 5.2 fusion.160
  955.9 7.1 fusion.53
  992.6 9.8 fusion.5
  1002.4 8.5 fusion.111
  1025.9 6.6 fusion.35
  1040.9 19.3 %multiply_bitcast_fusion.1 = f32[1,128,32,64]{3,2,1,0:T(8,128)} fusion(f32[1,128,32,64]{3,2,1,0:T(8,128)} %copy.487, f32[32,128,64]{2,0,1:T(8,128)} %get-tuple-element.936, f32[1,128,32,64]{3,2,1,0:T(8,128)} %copy-done.27, f32[32,128,64]{2,0,1:T(8,128)} %get-tuple-element.938, f32[1,128,32,64]{3,2,1,0:T(8,128)} %copy.463, ...), kind=kOutput, calls=%fused_computation.70 | output fusion | flops 40632320 | bytes 13656064 | tf_op jit(solution)/shard_map/transpose(jvp())/while/body/eval_jaxpr/jit(cumsum)/reduce_window_sum | solution.py:77
  (449 shorter events, 618.9 us)
Async XLA Ops:
  7.2 637.3 %all-gather.7.cloned.1.call-start = ((), (), s32[]{:S(2)}) async-start(), calls=%async_computation.1 | async-start | bytes 17825792 | tf_op jit(solution)/shard_map/all_gather | solution.py:19
  14.7 25.1 %copy-start.82 = (f32[128,32]{1,0:T(8,128)}, f32[128,32]{1,0:T(8,128)S(1)}, u32[]{:S(2)}) copy-start(f32[128,32]{1,0:T(8,128)S(1)} %copy.454) | copy-start | bytes 49156
  32.3 7.5 copy-start
  32.3 7.9 copy-start.17
  32.3 9.7 copy-start.22
  32.3 10.3 copy-start.26
  39.8 8.8 copy-start.27
  51.3 116.5 %copy-start.23 = (f32[32,128,64]{1,2,0:T(8,128)}, f32[32,128,64]{1,2,0:T(8,128)S(1)}, u32[]{:S(2)}) copy-start(f32[32,128,64]{1,2,0:T(8,128)S(1)} %copy.458) | copy-start | bytes 3145732
  150.3 494.2 %all-gather.5.cloned.1.call-start = ((), (), s32[]{:S(2)}) async-start(), calls=%async_computation | async-start | bytes 17825792 | tf_op jit(solution)/shard_map/all_gather | solution.py:19
  196.1 4.8 collective-permute-start
  204.5 33.0 %collective-permute-start = (f32[32,64,64]{2,1,0:T(8,128)}, f32[32,64,64]{2,1,0:T(8,128)S(1)}, u32[]{:S(2)}, u32[]{:S(2)}) collective-permute-start(f32[32,64,64]{2,1,0:T(8,128)} %convolution_add_fusion.16), channel_id=1, source_target_pairs={{0,1},{1,2},{2,3},{3,4},{4,5},{5,6},{6,7},{7,8},{8,9},{9,10},{10,1... | collective-permute-start | bytes 1572872 | tf_op jit(solution)/shard_map/while/body/eval_jaxpr/ppermute | solution.py:34
  241.2 35.9 %collective-permute-start = (f32[32,64,64]{2,1,0:T(8,128)}, f32[32,64,64]{2,1,0:T(8,128)S(1)}, u32[]{:S(2)}, u32[]{:S(2)}) collective-permute-start(f32[32,64,64]{2,1,0:T(8,128)} %convolution_add_fusion.16), channel_id=1, source_target_pairs={{0,1},{1,2},{2,3},{3,4},{4,5},{5,6},{6,7},{7,8},{8,9},{9,10},{10,1... | collective-permute-start | bytes 1572872 | tf_op jit(solution)/shard_map/while/body/eval_jaxpr/ppermute | solution.py:34
  280.8 16.5 %collective-permute-start = (f32[32,64,64]{2,1,0:T(8,128)}, f32[32,64,64]{2,1,0:T(8,128)S(1)}, u32[]{:S(2)}, u32[]{:S(2)}) collective-permute-start(f32[32,64,64]{2,1,0:T(8,128)} %convolution_add_fusion.16), channel_id=1, source_target_pairs={{0,1},{1,2},{2,3},{3,4},{4,5},{5,6},{6,7},{7,8},{8,9},{9,10},{10,1... | collective-permute-start | bytes 1572872 | tf_op jit(solution)/shard_map/while/body/eval_jaxpr/ppermute | solution.py:34
  300.9 16.5 %collective-permute-start = (f32[32,64,64]{2,1,0:T(8,128)}, f32[32,64,64]{2,1,0:T(8,128)S(1)}, u32[]{:S(2)}, u32[]{:S(2)}) collective-permute-start(f32[32,64,64]{2,1,0:T(8,128)} %convolution_add_fusion.16), channel_id=1, source_target_pairs={{0,1},{1,2},{2,3},{3,4},{4,5},{5,6},{6,7},{7,8},{8,9},{9,10},{10,1... | collective-permute-start | bytes 1572872 | tf_op jit(solution)/shard_map/while/body/eval_jaxpr/ppermute | solution.py:34
  321.1 22.3 %collective-permute-start = (f32[32,64,64]{2,1,0:T(8,128)}, f32[32,64,64]{2,1,0:T(8,128)S(1)}, u32[]{:S(2)}, u32[]{:S(2)}) collective-permute-start(f32[32,64,64]{2,1,0:T(8,128)} %convolution_add_fusion.16), channel_id=1, source_target_pairs={{0,1},{1,2},{2,3},{3,4},{4,5},{5,6},{6,7},{7,8},{8,9},{9,10},{10,1... | collective-permute-start | bytes 1572872 | tf_op jit(solution)/shard_map/while/body/eval_jaxpr/ppermute | solution.py:34
  347.0 48.5 %collective-permute-start = (f32[32,64,64]{2,1,0:T(8,128)}, f32[32,64,64]{2,1,0:T(8,128)S(1)}, u32[]{:S(2)}, u32[]{:S(2)}) collective-permute-start(f32[32,64,64]{2,1,0:T(8,128)} %convolution_add_fusion.16), channel_id=1, source_target_pairs={{0,1},{1,2},{2,3},{3,4},{4,5},{5,6},{6,7},{7,8},{8,9},{9,10},{10,1... | collective-permute-start | bytes 1572872 | tf_op jit(solution)/shard_map/while/body/eval_jaxpr/ppermute | solution.py:34
  399.2 37.8 %collective-permute-start = (f32[32,64,64]{2,1,0:T(8,128)}, f32[32,64,64]{2,1,0:T(8,128)S(1)}, u32[]{:S(2)}, u32[]{:S(2)}) collective-permute-start(f32[32,64,64]{2,1,0:T(8,128)} %convolution_add_fusion.16), channel_id=1, source_target_pairs={{0,1},{1,2},{2,3},{3,4},{4,5},{5,6},{6,7},{7,8},{8,9},{9,10},{10,1... | collective-permute-start | bytes 1572872 | tf_op jit(solution)/shard_map/while/body/eval_jaxpr/ppermute | solution.py:34
  440.6 16.9 %collective-permute-start = (f32[32,64,64]{2,1,0:T(8,128)}, f32[32,64,64]{2,1,0:T(8,128)S(1)}, u32[]{:S(2)}, u32[]{:S(2)}) collective-permute-start(f32[32,64,64]{2,1,0:T(8,128)} %convolution_add_fusion.16), channel_id=1, source_target_pairs={{0,1},{1,2},{2,3},{3,4},{4,5},{5,6},{6,7},{7,8},{8,9},{9,10},{10,1... | collective-permute-start | bytes 1572872 | tf_op jit(solution)/shard_map/while/body/eval_jaxpr/ppermute | solution.py:34
  461.2 36.3 %collective-permute-start = (f32[32,64,64]{2,1,0:T(8,128)}, f32[32,64,64]{2,1,0:T(8,128)S(1)}, u32[]{:S(2)}, u32[]{:S(2)}) collective-permute-start(f32[32,64,64]{2,1,0:T(8,128)} %convolution_add_fusion.16), channel_id=1, source_target_pairs={{0,1},{1,2},{2,3},{3,4},{4,5},{5,6},{6,7},{7,8},{8,9},{9,10},{10,1... | collective-permute-start | bytes 1572872 | tf_op jit(solution)/shard_map/while/body/eval_jaxpr/ppermute | solution.py:34
  501.2 17.2 %collective-permute-start = (f32[32,64,64]{2,1,0:T(8,128)}, f32[32,64,64]{2,1,0:T(8,128)S(1)}, u32[]{:S(2)}, u32[]{:S(2)}) collective-permute-start(f32[32,64,64]{2,1,0:T(8,128)} %convolution_add_fusion.16), channel_id=1, source_target_pairs={{0,1},{1,2},{2,3},{3,4},{4,5},{5,6},{6,7},{7,8},{8,9},{9,10},{10,1... | collective-permute-start | bytes 1572872 | tf_op jit(solution)/shard_map/while/body/eval_jaxpr/ppermute | solution.py:34
  522.1 17.2 %collective-permute-start = (f32[32,64,64]{2,1,0:T(8,128)}, f32[32,64,64]{2,1,0:T(8,128)S(1)}, u32[]{:S(2)}, u32[]{:S(2)}) collective-permute-start(f32[32,64,64]{2,1,0:T(8,128)} %convolution_add_fusion.16), channel_id=1, source_target_pairs={{0,1},{1,2},{2,3},{3,4},{4,5},{5,6},{6,7},{7,8},{8,9},{9,10},{10,1... | collective-permute-start | bytes 1572872 | tf_op jit(solution)/shard_map/while/body/eval_jaxpr/ppermute | solution.py:34
  543.0 17.2 %collective-permute-start = (f32[32,64,64]{2,1,0:T(8,128)}, f32[32,64,64]{2,1,0:T(8,128)S(1)}, u32[]{:S(2)}, u32[]{:S(2)}) collective-permute-start(f32[32,64,64]{2,1,0:T(8,128)} %convolution_add_fusion.16), channel_id=1, source_target_pairs={{0,1},{1,2},{2,3},{3,4},{4,5},{5,6},{6,7},{7,8},{8,9},{9,10},{10,1... | collective-permute-start | bytes 1572872 | tf_op jit(solution)/shard_map/while/body/eval_jaxpr/ppermute | solution.py:34
  563.9 17.2 %collective-permute-start = (f32[32,64,64]{2,1,0:T(8,128)}, f32[32,64,64]{2,1,0:T(8,128)S(1)}, u32[]{:S(2)}, u32[]{:S(2)}) collective-permute-start(f32[32,64,64]{2,1,0:T(8,128)} %convolution_add_fusion.16), channel_id=1, source_target_pairs={{0,1},{1,2},{2,3},{3,4},{4,5},{5,6},{6,7},{7,8},{8,9},{9,10},{10,1... | collective-permute-start | bytes 1572872 | tf_op jit(solution)/shard_map/while/body/eval_jaxpr/ppermute | solution.py:34
  584.8 17.2 %collective-permute-start = (f32[32,64,64]{2,1,0:T(8,128)}, f32[32,64,64]{2,1,0:T(8,128)S(1)}, u32[]{:S(2)}, u32[]{:S(2)}) collective-permute-start(f32[32,64,64]{2,1,0:T(8,128)} %convolution_add_fusion.16), channel_id=1, source_target_pairs={{0,1},{1,2},{2,3},{3,4},{4,5},{5,6},{6,7},{7,8},{8,9},{9,10},{10,1... | collective-permute-start | bytes 1572872 | tf_op jit(solution)/shard_map/while/body/eval_jaxpr/ppermute | solution.py:34
  602.1 29.0 %copy-start.2 = (f32[32,64,64]{2,1,0:T(8,128)}, f32[32,64,64]{2,1,0:T(8,128)S(1)}, u32[]{:S(2)}) copy-start(f32[32,64,64]{2,1,0:T(8,128)S(1)} %get-tuple-element.809) | copy-start | bytes 1572868
  795.7 101.9 %copy-start.52 = (f32[32,64,128]{2,1,0:T(8,128)}, f32[32,64,128]{2,1,0:T(8,128)S(1)}, u32[]{:S(2)}) copy-start(f32[32,64,128]{2,1,0:T(8,128)S(1)} %fusion.144) | copy-start | bytes 3145732
  868.2 7.5 copy-start.44
  930.3 7.1 copy-start.6
  930.3 7.1 copy-start.45
  955.9 7.1 copy-start.51
  955.9 7.1 copy-start.70
  1025.7 6.8 copy-start.31
  (89 other events, 268.7 us)
Sparse Core Ops, SparseCore 0:
  150.4 143.6 all-gather.6
  296.2 157.8 all-gather.4
where the time goes:
time: 1090 us; the launch traced here: 1080 us
  matrix products  371 us (34%)
  starting transfers between devices  319 us (29%)
  local copies, waits for them, and re-layouts  262 us (24%)
  other arithmetic  72.5 us (7%)
  waiting for transfers between devices  36.2 us (3%)
  between operations  15.8 us (1%)
    ppermute x15, starting transfers between devices, shifted(): return lax.ppermute(x, axis, pairs)  318 us
    dot_general x30, matrix products, compose(): return jnp.einsum('hij,hjk->hik', left, right, precision=precise)  101 us
    dynamic_slice x30, local copies, waits for them, and re-layouts, one(): lax.dynamic_index_in_dim(a, source, 0, False)  73.2 us
    dot_general x18, matrix products, unit_lower_inverse(): jnp.einsum('hts,hsu->htu', result, power, precision=precise)  66.5 us
    dot_general x18, matrix products, unit_lower_inverse(): power = jnp.einsum('hts,hsu->htu', power, power, precision=precise)  65.3 us
    ppermute x15, waiting for transfers between devices, shifted(): return lax.ppermute(x, axis, pairs)  36.1 us
    unnamed x191, local copies, waits for them, and re-layouts  30.5 us
  transfers between devices with their start and end apart: 17, of which 15 were waited for; matrix products, arithmetic and copies ran while one was open for 12% of the time, Pallas kernels for 0%

commit v1 on v0

v1 whole, which is shorter than its diff:
```python
import functools

import jax
import jax.numpy as jnp
from jax import lax
from jax.experimental import pallas as pl
from jax.experimental.pallas import tpu as pltpu
from jax.sharding import PartitionSpec as P

HS = 64
LANES = 128
ROWS = 128
DECAY_SCALE = 0.6065306597126334
MESH = pl.DeviceIdType.MESH
NN = (((1,), (0,)), ((), ()))
NT = (((1,), (1,)), ((), ()))
TN = (((0,), (0,)), ((), ()))
F32 = jnp.float32
BF16 = jnp.bfloat16


def dot(x, y, dims):
    return lax.dot_general(x, y, dims, preferred_element_type=F32)


def split(x):
    if x.dtype == BF16:
        return (x, None)
    high = x.astype(BF16)
    return (high, (x - high.astype(F32)).astype(BF16))


def mm(x, y, dims=NN):
    total = dot(x[0], y[0], dims)
    if y[1] is not None:
        total = total + dot(x[0], y[1], dims)
    if x[1] is not None:
        total = total + dot(x[1], y[0], dims)
    return total


def masked(x, mask):
    return tuple(None if part is None else part * mask for part in x)


def stack(x, y):
    low = None
    if x[1] is not None or y[1] is not None:
        low = jnp.concatenate(
            [jnp.zeros_like(z[0]) if z[1] is None else z[1] for z in (x, y)], axis=0
        )
    return (jnp.concatenate([x[0], y[0]], axis=0), low)


def exact_sum(ones, x, dims=NN, left=True):
    high = x.astype(BF16)
    rest = x - high.astype(F32)
    mid = rest.astype(BF16)
    low = (rest - mid.astype(F32)).astype(BF16)
    parts = [dot(ones, z, dims) if left else dot(z, ones, dims) for z in (low, mid, high)]
    return parts[0] + parts[1] + parts[2]


def iotas(rows, columns):
    return (
        lax.broadcasted_iota(jnp.int32, (rows, columns), 0),
        lax.broadcasted_iota(jnp.int32, (rows, columns), 1),
    )


def lane_masks():
    lane = lax.broadcasted_iota(jnp.int32, (1, LANES), 1)
    first = (lane < HS).astype(F32)
    return (first.astype(BF16), (1.0 - first).astype(BF16))


def own_lanes(x0, x1):
    lane = lax.broadcasted_iota(jnp.int32, x0.shape, 1)
    return jnp.where(lane % LANES < HS, x0, x1)


def same_head():
    row, column = iotas(LANES, LANES)
    return row // HS == column // HS


def prepare(r_ref, d_ref, k_ref, x_ref, rate_ref):
    row, column = iotas(ROWS, ROWS)
    sig = jax.nn.sigmoid(d_ref[...].astype(F32))
    log_decay = -DECAY_SCALE * sig
    cum = exact_sum((row >= column).astype(F32).astype(BF16), log_decay)
    x = x_ref[...].astype(F32)
    ones = same_head().astype(F32).astype(BF16)
    inv = lax.rsqrt(exact_sum(ones, x * x, left=False) + 1e-06)
    direction = x * inv
    rate = rate_ref[...].astype(F32)
    ec, ep, en = jnp.exp(cum), jnp.exp(cum - log_decay), jnp.exp(-cum)
    take = -direction * ep
    query = r_ref[...].astype(F32) * ec
    give = direction * rate * en
    key = k_ref[...].astype(F32) * en
    return sig, inv, direction, rate, ec, ep, en, take, query, give, key, ones


def invert(lowers):
    row, column = iotas(ROWS, ROWS)
    eye = (row == column).astype(F32)
    results = [
        eye + jnp.where((row // 2 == column // 2), lower, 0.0) for lower in lowers
    ]
    size = 2
    while size < ROWS:
        here = (row // (2 * size) == column // (2 * size)) & (row // size != column // size)
        splits = [split(x) for x in results]
        offs = [split(jnp.where(here, lower, 0.0)) for lower in lowers]
        halves = [split(mm(x, off)) for x, off in zip(splits, offs)]
        results = [x + mm(h, s) for x, h, s in zip(results, halves, splits)]
        size *= 2
    return results


def compact(x):
    x = jnp.where(same_head(), x, 0.0)
    return x[:HS] + x[HS:]


def expand(x):
    return jnp.where(same_head(), jnp.concatenate([x, x], axis=0), 0.0)


def local_kernel(
    r_ref, d_ref, k_ref, v_ref, x_ref, rate_ref, g_ref,
    send_ref, u_ref, y_ref, w_ref, xx_ref, dv_ref, rr_ref,
):
    _, _, _, _, ec, _, _, take, query, give, key, _ = prepare(
        r_ref, d_ref, k_ref, x_ref, rate_ref
    )
    row, column = iotas(2 * ROWS, 2 * ROWS)
    t_in, s_in = row % ROWS, column % ROWS
    lower = t_in - s_in >= jnp.where(row < ROWS, 1, 0)
    upper = s_in - t_in >= jnp.where(column < ROWS, 1, 0)
    values, grads = (v_ref[...], None), (g_ref[...], None)
    take_s, query_s, give_s, key_s = split(take), split(query), split(give), split(key)
    aq, gk = stack(take_s, query_s), stack(give_s, key_s)
    masks = lane_masks()
    forward = [jnp.where(lower, mm(masked(aq, m), gk, NT), 0.0) for m in masks]
    backward = [split(jnp.where(upper, mm(masked(gk, m), aq, NT), 0.0)) for m in masks]
    inverses = invert([f[:ROWS, :ROWS] for f in forward])
    bv = own_lanes(*[mm(split(f[:ROWS, ROWS:]), values) for f in forward])
    ptg = own_lanes(
        *[mm((b[0][:, ROWS:], b[1][:, ROWS:]), grads) for b in backward]
    )
    bv_s, ptg_s = split(bv), split(ptg[:ROWS])

    def beside(x, y):
        return tuple(jnp.concatenate([p, q], axis=1) for p, q in zip(x, y))

    yu = own_lanes(*[mm(split(m), beside(take_s, bv_s)) for m in inverses])
    xw = own_lanes(*[mm(split(m.T), beside(give_s, ptg_s)) for m in inverses])
    y_ref[...] = yu[:, :LANES]
    u_ref[...] = yu[:, LANES:]
    xx_ref[...] = xw[:, :LANES]
    w_ref[...] = xw[:, LANES:]
    xw_s = split(xw)
    bt = own_lanes(
        *[mm((b[0][ROWS:, :ROWS], b[1][ROWS:, :ROWS]), xw_s) for b in backward]
    )
    rr_ref[...] = bt[:, :LANES] + key
    dv_ref[...] = ptg[ROWS:] + bt[:, LANES:]
    yu_s = split(yu)
    last = ec[ROWS - 1 :, :]
    r128, c128 = iotas(LANES, LANES)
    eye = (r128 == c128).astype(F32)
    y_s = tuple(p[:, :LANES] for p in yu_s)
    u_s = tuple(p[:, LANES:] for p in yu_s)
    w_s = tuple(p[:, LANES:] for p in xw_s)
    send_ref[0, 0] = compact((eye + mm(y_s, give_s, TN)) * last)
    send_ref[0, 1] = compact((mm(u_s, give_s, TN) + mm(values, key_s, TN)) * last)
    send_ref[0, 2] = compact(mm(grads, query_s, TN) + mm(w_s, take_s, TN))


def scan_kernel(
    n, pairs, own_ref, start_ref, end_ref,
    got, starts, ends, sent_sem, got_sem, s_sent, s_got, d_sent, d_got,
):
    me = lax.axis_index("ctx")
    barrier = pltpu.get_barrier_semaphore()
    for j in range(1, n):
        pl.semaphore_signal(
            barrier, inc=1, device_id={"ctx": lax.rem(me + j, n)}, device_id_type=MESH
        )
    pl.semaphore_wait(barrier, n - 1)

    def collect(source, owner):
        return pltpu.make_async_remote_copy(
            src_ref=own_ref.at[owner],
            dst_ref=got.at[source],
            send_sem=sent_sem.at[owner],
            recv_sem=got_sem.at[source],
            device_id={"ctx": owner},
            device_id_type=MESH,
        )

    def give_back(held, target_ref, sent, received, target, owner):
        return pltpu.make_async_remote_copy(
            src_ref=held.at[target],
            dst_ref=target_ref.at[owner],
            send_sem=sent.at[target],
            recv_sem=received.at[owner],
            device_id={"ctx": target},
            device_id_type=MESH,
        )

    def send(j, carry):
        owner = lax.rem(me + j, pairs)

        @pl.when(owner != me)
        def _():
            collect(me, owner).start()

        return carry

    lax.fori_loop(0, pairs, send, 0)

    def scan():
        got[me] = own_ref[me]

        def step(i, carry):
            state, adjoint = carry
            back = n - 1 - i

            @pl.when(i < n // 2)
            def _():
                for source in (i, back):
                    @pl.when(source != me)
                    def _():
                        collect(source, me).wait_recv()

            starts[i] = state
            ends[back] = adjoint
            start_copy = give_back(starts, start_ref, s_sent, s_got, i, me)
            end_copy = give_back(ends, end_ref, d_sent, d_got, back, me)

            @pl.when(i != me)
            def _():
                start_copy.start()

            @pl.when(back != me)
            def _():
                end_copy.start()

            moved = mm(split(state), split(expand(got[i, 0]))) + got[i, 1]
            moved_back = (
                mm(split(adjoint), split(expand(got[back, 0])), NT) + got[back, 2]
            )
            return moved, moved_back

        zero = jnp.zeros((HS, LANES), F32)
        lax.fori_loop(0, n, step, (zero, zero))
        start_ref[me] = starts[me]
        end_ref[me] = ends[me]

        def drain(i, carry):
            @pl.when(i != me)
            def _():
                give_back(starts, start_ref, s_sent, s_got, i, me).wait_send()
                give_back(ends, end_ref, d_sent, d_got, i, me).wait_send()

            return carry

        lax.fori_loop(0, n, drain, 0)

    if n == pairs:
        scan()
    else:
        pl.when(me < pairs)(scan)

    def finish(owner, carry):
        @pl.when(owner != me)
        def _():
            collect(me, owner).wait_send()
            give_back(starts, start_ref, s_sent, s_got, me, owner).wait_recv()
            give_back(ends, end_ref, d_sent, d_got, me, owner).wait_recv()

        return carry

    lax.fori_loop(0, pairs, finish, 0)


def grad_kernel(
    r_ref, d_ref, k_ref, v_ref, x_ref, rate_ref, g_ref,
    start_ref, end_ref, u_ref, y_ref, w_ref, xx_ref, dv_ref, rr_ref,
    gr_ref, gd_ref, gk_ref, gv_ref, gx_ref, grate_ref,
):
    sig, inv, direction, rate, ec, ep, en, take, query, give, key, ones = prepare(
        r_ref, d_ref, k_ref, x_ref, rate_ref
    )
    row, column = iotas(2 * ROWS, 2 * ROWS)
    t_in, s_in = row % ROWS, column % ROWS
    lower = t_in - s_in >= jnp.where(row < ROWS, 0, 1)
    upper = s_in - t_in >= jnp.where(column < ROWS, 0, 1)
    values, grads = (v_ref[...], None), (g_ref[...], None)
    start = expand(start_ref[0])
    after = expand(end_ref[0] * ec[ROWS - 1 :, :])
    start_s, after_s = split(start), split(after)
    u = u_ref[...] + mm(split(y_ref[...]), start_s, NT)
    w = w_ref[...] + mm(split(xx_ref[...]), after_s, NT)
    dv = dv_ref[...] + mm(split(rr_ref[...]), after_s, NT)
    gv_ref[...] = dv.astype(BF16)
    gw, uv = stack(grads, split(w)), stack(split(u), values)
    qa, gk = stack(split(query), split(take)), stack(split(give), split(key))
    masks = lane_masks()
    forward = [split(jnp.where(lower, mm(masked(gw, m), uv, NT), 0.0)) for m in masks]
    backward = [split(jnp.where(upper, mm(masked(uv, m), gw, NT), 0.0)) for m in masks]
    uvd = mm(uv, after_s)
    dqa = mm(gw, start_s) + own_lanes(*[mm(f, gk) for f in forward])
    dgk = uvd + own_lanes(*[mm(b, qa) for b in backward])
    dq, da, dg, dk = dqa[:ROWS], dqa[ROWS:], dgk[:ROWS], dgk[ROWS:]
    gr_ref[...] = (dq * ec).astype(BF16)
    gk_ref[...] = (dk * en).astype(BF16)
    dg_plain = dg * en
    grate_ref[...] = (dg_plain * direction).astype(BF16)
    d_dir = dg_plain * rate - da * ep
    along = exact_sum(ones, direction * d_dir, left=False)
    gx_ref[...] = (inv * (d_dir - direction * along)).astype(BF16)
    d_previous = take * da
    d_cum = query * dq - give * dg - key * dk + d_previous
    at_end = (
        jnp.sum(start * after, axis=0, keepdims=True)
        + jnp.sum(give * uvd[:ROWS] + key * uvd[ROWS:], axis=0, keepdims=True)
    )
    r128, c128 = iotas(ROWS, ROWS)
    d_log = exact_sum((r128 <= c128).astype(F32).astype(BF16), d_cum) - d_previous + at_end
    gd_ref[...] = (d_log * (-DECAY_SCALE) * sig * (1.0 - sig)).astype(BF16)


def per_device(*arrays):
    rows, width = arrays[0].shape
    pairs = width // LANES
    n = lax.axis_size("ctx")
    tokens = pl.BlockSpec((rows, LANES), lambda i: (0, i))
    wide = jax.ShapeDtypeStruct((rows, width), F32)
    params = pltpu.CompilerParams(vmem_limit_bytes=48 * 1024 * 1024)
    local = pl.pallas_call(
        local_kernel,
        grid=(pairs,),
        in_specs=[tokens] * 7,
        out_specs=[pl.BlockSpec((1, 3, HS, LANES), lambda i: (i, 0, 0, 0))] + [tokens] * 6,
        out_shape=[jax.ShapeDtypeStruct((pairs, 3, HS, LANES), F32)] + [wide] * 6,
        compiler_params=params,
    )(*arrays)
    state = jax.ShapeDtypeStruct((pairs, HS, LANES), F32)
    vmem = pl.BlockSpec(memory_space=pltpu.VMEM)
    start, end = pl.pallas_call(
        functools.partial(scan_kernel, n, pairs),
        in_specs=[vmem],
        out_specs=[vmem, vmem],
        out_shape=[state, state],
        scratch_shapes=[
            pltpu.VMEM((n, 3, HS, LANES), F32),
            pltpu.VMEM((n, HS, LANES), F32),
            pltpu.VMEM((n, HS, LANES), F32),
            pltpu.SemaphoreType.DMA((pairs,)),
            pltpu.SemaphoreType.DMA((n,)),
            pltpu.SemaphoreType.DMA((n,)),
            pltpu.SemaphoreType.DMA((pairs,)),
            pltpu.SemaphoreType.DMA((n,)),
            pltpu.SemaphoreType.DMA((pairs,)),
        ],
        compiler_params=pltpu.CompilerParams(
            collective_id=0, has_side_effects=True, vmem_limit_bytes=48 * 1024 * 1024
        ),
    )(local[0])
    one = pl.BlockSpec((1, HS, LANES), lambda i: (i, 0, 0))
    return tuple(
        pl.pallas_call(
            grad_kernel,
            grid=(pairs,),
            in_specs=[tokens] * 7 + [one, one] + [tokens] * 6,
            out_specs=[tokens] * 6,
            out_shape=[jax.ShapeDtypeStruct((rows, width), BF16)] * 6,
            compiler_params=params,
        )(*arrays, start, end, *local[1:])
    )


def solution(mesh):
    placed = P(("groups", "ctx"), None)
    return jax.shard_map(
        per_device,
        mesh=mesh,
        in_specs=(placed,) * 7,
        out_specs=(placed,) * 6,
        check_vma=False,
    )
```

time: 1090 us -> 171 us (0.16); the launches traced: 1080 us -> 171 us
  matrix products: 371 us -> 0 us
  starting transfers between devices: 319 us -> 0 us
  local copies, waits for them, and re-layouts: 262 us -> 9.12 us
  Pallas kernels: 0 us -> 161 us
  other arithmetic: 72.5 us -> 0 us
  waiting for transfers between devices: 36.2 us -> 0 us
  between operations: 15.8 us -> 0.73 us
    dot_general x104 -> x0, matrix products: 371 us -> none  [the longest x30 101 us: compose(): return jnp.einsum('hij,hjk->hik', left, right, precision=precise)]
    ppermute x15 -> x0, starting transfers between devices: 318 us -> none  [shifted(): return lax.ppermute(x, axis, pairs)]
    pallas_call x0 -> x3, Pallas kernels: none -> 161 us  [the longest x1 70.7 us: per_device(): pl.pallas_call(functools.partial(scan_kernel, n, pairs), in_specs=[vmem],...]
    dynamic_slice x32 -> x0, local copies, waits for them, and re-layouts: 79.6 us -> none  [the longest x30 73.2 us: one(): lax.dynamic_index_in_dim(a, source, 0, False)]
    dot_general x14 -> x0, local copies, waits for them, and re-layouts: 55.8 us -> none  [the longest x2 8.27 us: block_step(): jnp.einsum('hsi,hsj->hij', value_rows, key_scaled * final_decay, precisio...]
    ppermute x15 -> x0, waiting for transfers between devices: 36.1 us -> none  [shifted(): return lax.ppermute(x, axis, pairs)]
    while x48 -> x0, local copies, waits for them, and re-layouts: 24.3 us -> none
    mul x8 -> x0, local copies, waits for them, and re-layouts: 23.1 us -> none  [the longest x2 5.52 us: prepare(): log_decay = -DECAY_SCALE * jax.nn.sigmoid(headed(decay_logit))]
  transfers between devices with their start and end apart: 17 -> 0, of which waited for: 15 -> 0; matrix products, arithmetic and copies ran while one was open for 12% -> 0% of each run, Pallas kernels for 0% -> 0%
where the time goes in v1:
time: 171 us
  Pallas kernels  161 us (94%)
  local copies, waits for them, and re-layouts  9.12 us (5%)
    pallas_call x1, Pallas kernels, per_device(): pl.pallas_call(functools.partial(scan_kernel, n, pairs), in_specs=[vmem],...  70.7 us
    pallas_call x1, Pallas kernels, per_device(): pl.pallas_call(local_kernel, grid=(pairs,), in_specs=[tokens] * 7, out_sp...  58.9 us
    pallas_call x1, Pallas kernels, per_device(): pl.pallas_call(grad_kernel, grid=(pairs,), in_specs=[tokens] * 7 + [one,...  31.4 us
    unnamed x28, local copies, waits for them, and re-layouts  9.12 us

profile of v1, /device:TPU:0, one launch (start us, length us, event | category | flops | bytes accessed | tf_op | source)
XLA Modules:
  0.0 170.8 jit_solution(4914416821516283688)
XLA Ops:
  0.6 0.0 copy-start
  0.6 1.0 copy-done
  1.7 0.0 copy-start.2
  1.7 1.0 copy-done.2
  2.7 0.0 copy-start.4
  2.7 1.0 copy-done.4
  3.8 0.0 copy-start.6
  3.8 1.0 copy-done.6
  4.8 0.0 copy-start.8
  4.8 1.0 copy-done.8
  5.8 0.0 copy-start.10
  5.8 1.0 copy-done.10
  6.9 0.0 copy-start.11
  6.9 1.0 copy-done.11
  7.9 0.0 copy-start.7
  7.9 0.0 copy-start.9
  7.9 58.9 %shard_map.118 = (f32[16,3,64,128]{3,2,1,0:T(8,128)}, f32[128,2048]{1,0:T(8,128)S(1)}, f32[128,2048]{1,0:T(8,128)S(1)}, f32[128,2048]{1,0:T(8,128)}, f32[128,204...) custom-call(bf16[128,2048]{1,0:T(8,128)(2,1)S(1)} %copy-done, bf16[128,2048]{1,0:T(8,128)(2,1)S(1)} %copy-done.2, ...), custom_call_target="tpu_custom_call" | custom-call | tf_op jit(solution)/shard_map/pallas_call | solution.py:344
  66.8 0.0 copy-start.13
  66.8 0.0 copy-start.1
  66.8 0.0 copy-start.3
  66.8 0.0 copy-start.5
  66.8 0.0 copy-start.12
  66.8 1.8 %copy-done.12 = f32[16,3,64,128]{3,2,1,0:T(8,128)S(1)} copy-done((f32[16,3,64,128]{3,2,1,0:T(8,128)S(1)}, f32[16,3,64,128]{3,2,1,0:T(8,128)}, u32[]{:S(2)}) %copy-start.12) | copy-done | bytes 1572888
  68.6 70.7 %shard_map.119 = (f32[16,64,128]{2,1,0:T(8,128)S(1)}, f32[16,64,128]{2,1,0:T(8,128)S(1)}) custom-call(f32[16,3,64,128]{3,2,1,0:T(8,128)S(1)} %copy-done.12), custom_call_target="tpu_custom_call" | custom-call | tf_op jit(solution)/shard_map/pallas_call | solution.py:354
  139.3 0.0 copy-done.13
  139.3 0.0 copy-done.7
  139.3 0.0 copy-done.9
  139.3 0.0 copy-done.1
  139.3 0.0 copy-done.3
  139.4 0.0 copy-done.5
  139.4 31.4 %shard_map.120 = (bf16[128,2048]{1,0:T(8,128)(2,1)}, bf16[128,2048]{1,0:T(8,128)(2,1)}, bf16[128,2048]{1,0:T(8,128)(2,1)}, bf16[128,2048]{1,0:T(8,128)(2,1)}, bf...) custom-call(bf16[128,2048]{1,0:T(8,128)(2,1)S(1)} %copy-done.1, bf16[128,2048]{1,0:T(8,128)(2,1)S(1)} %copy-done.3, ...), custom_call_target="tpu_custom_call" | custom-call | tf_op jit(solution)/shard_map/pallas_call | solution.py:376
Async XLA Ops:
  0.6 1.0 copy-start
  1.7 1.0 copy-start.2
  2.7 1.0 copy-start.4
  3.8 1.0 copy-start.6
  4.8 1.0 copy-start.8
  5.8 1.0 copy-start.10
  6.9 1.0 copy-start.11
  7.9 131.4 %copy-start.7 = (bf16[128,2048]{1,0:T(8,128)(2,1)S(1)}, bf16[128,2048]{1,0:T(8,128)(2,1)}, u32[]{:S(2)}) copy-start(bf16[128,2048]{1,0:T(8,128)(2,1)} %v_ref.3) | copy-start | bytes 1572868
  7.9 131.4 %copy-start.9 = (bf16[128,2048]{1,0:T(8,128)(2,1)S(1)}, bf16[128,2048]{1,0:T(8,128)(2,1)}, u32[]{:S(2)}) copy-start(bf16[128,2048]{1,0:T(8,128)(2,1)} %x_ref.3) | copy-start | bytes 1572868
  66.8 72.5 %copy-start.13 = (f32[128,2048]{1,0:T(8,128)}, f32[128,2048]{1,0:T(8,128)S(1)}, u32[]{:S(2)}) copy-start(f32[128,2048]{1,0:T(8,128)S(1)} %get-tuple-element.19.y_ref) | copy-start | bytes 3145732
  66.8 72.5 %copy-start.1 = (bf16[128,2048]{1,0:T(8,128)(2,1)S(1)}, bf16[128,2048]{1,0:T(8,128)(2,1)}, u32[]{:S(2)}) copy-start(bf16[128,2048]{1,0:T(8,128)(2,1)} %r_ref.3) | copy-start | bytes 1572868
  66.8 72.6 %copy-start.3 = (bf16[128,2048]{1,0:T(8,128)(2,1)S(1)}, bf16[128,2048]{1,0:T(8,128)(2,1)}, u32[]{:S(2)}) copy-start(bf16[128,2048]{1,0:T(8,128)(2,1)} %d_ref.3) | copy-start | bytes 1572868
  66.8 72.6 %copy-start.5 = (bf16[128,2048]{1,0:T(8,128)(2,1)S(1)}, bf16[128,2048]{1,0:T(8,128)(2,1)}, u32[]{:S(2)}) copy-start(bf16[128,2048]{1,0:T(8,128)(2,1)} %k_ref.3) | copy-start | bytes 1572868
  66.8 1.8 %copy-start.12 = (f32[16,3,64,128]{3,2,1,0:T(8,128)S(1)}, f32[16,3,64,128]{3,2,1,0:T(8,128)}, u32[]{:S(2)}) copy-start(f32[16,3,64,128]{3,2,1,0:T(8,128)} %get-tuple-element.15.own_ref) | copy-start | bytes 4718596

commit v2 on v1

--- a/solution.py
+++ b/solution.py
@@ -10,6 +10,8 @@
 HS = 64
 LANES = 128
 ROWS = 128
+LOCAL = 4
+LATER = 4
 DECAY_SCALE = 0.6065306597126334
 MESH = pl.DeviceIdType.MESH
 NN = (((1,), (0,)), ((), ()))
@@ -128,10 +130,11 @@
     return jnp.where(same_head(), jnp.concatenate([x, x], axis=0), 0.0)
 
 
-def local_kernel(
-    r_ref, d_ref, k_ref, v_ref, x_ref, rate_ref, g_ref,
-    send_ref, u_ref, y_ref, w_ref, xx_ref, dv_ref, rr_ref,
-):
+def beside(x, y):
+    return tuple(jnp.concatenate([p, q], axis=1) for p, q in zip(x, y))
+
+
+def local_first(r_ref, d_ref, k_ref, v_ref, x_ref, rate_ref, g_ref):
     _, _, _, _, ec, _, _, take, query, give, key, _ = prepare(
         r_ref, d_ref, k_ref, x_ref, rate_ref
     )
@@ -143,40 +146,61 @@
     take_s, query_s, give_s, key_s = split(take), split(query), split(give), split(key)
     aq, gk = stack(take_s, query_s), stack(give_s, key_s)
     masks = lane_masks()
-    forward = [jnp.where(lower, mm(masked(aq, m), gk, NT), 0.0) for m in masks]
+    forward = [
+        jnp.where(lower[:ROWS], mm(masked(take_s, m), gk, NT), 0.0) for m in masks
+    ]
     backward = [split(jnp.where(upper, mm(masked(gk, m), aq, NT), 0.0)) for m in masks]
-    inverses = invert([f[:ROWS, :ROWS] for f in forward])
-    bv = own_lanes(*[mm(split(f[:ROWS, ROWS:]), values) for f in forward])
+    bv = own_lanes(*[mm(split(f[:, ROWS:]), values) for f in forward])
     ptg = own_lanes(
         *[mm((b[0][:, ROWS:], b[1][:, ROWS:]), grads) for b in backward]
     )
-    bv_s, ptg_s = split(bv), split(ptg[:ROWS])
-
-    def beside(x, y):
-        return tuple(jnp.concatenate([p, q], axis=1) for p, q in zip(x, y))
-
-    yu = own_lanes(*[mm(split(m), beside(take_s, bv_s)) for m in inverses])
-    xw = own_lanes(*[mm(split(m.T), beside(give_s, ptg_s)) for m in inverses])
-    y_ref[...] = yu[:, :LANES]
-    u_ref[...] = yu[:, LANES:]
-    xx_ref[...] = xw[:, :LANES]
-    w_ref[...] = xw[:, LANES:]
+    lowers = [f[:, :ROWS] for f in forward]
+    take_bv = beside(take_s, split(bv))
+    give_ptg = beside(give_s, split(ptg[:ROWS]))
+    bts = [(b[0][ROWS:, :ROWS], b[1][ROWS:, :ROWS]) for b in backward]
+    return lowers, (
+        take_bv, give_ptg, bts, ptg[ROWS:], key, values, grads,
+        take_s, query_s, give_s, key_s, ec[ROWS - 1 :, :],
+    )
+
+
+def local_second(inverses, kept, at, send_ref, u_ref, y_ref, w_ref, xx_ref, dv_ref, rr_ref):
+    (
+        take_bv, give_ptg, bts, qtg, key, values, grads,
+        take_s, query_s, give_s, key_s, last,
+    ) = kept
+    lanes = slice(at * LANES, (at + 1) * LANES)
+    yu = own_lanes(*[mm(split(m), take_bv) for m in inverses])
+    xw = own_lanes(*[mm(split(m.T), give_ptg) for m in inverses])
+    y_ref[:, lanes] = yu[:, :LANES]
+    u_ref[:, lanes] = yu[:, LANES:]
+    xx_ref[:, lanes] = xw[:, :LANES]
+    w_ref[:, lanes] = xw[:, LANES:]
     xw_s = split(xw)
-    bt = own_lanes(
-        *[mm((b[0][ROWS:, :ROWS], b[1][ROWS:, :ROWS]), xw_s) for b in backward]
-    )
-    rr_ref[...] = bt[:, :LANES] + key
-    dv_ref[...] = ptg[ROWS:] + bt[:, LANES:]
+    bt = own_lanes(*[mm(b, xw_s) for b in bts])
+    rr_ref[:, lanes] = bt[:, :LANES] + key
+    dv_ref[:, lanes] = qtg + bt[:, LANES:]
     yu_s = split(yu)
-    last = ec[ROWS - 1 :, :]
     r128, c128 = iotas(LANES, LANES)
     eye = (r128 == c128).astype(F32)
     y_s = tuple(p[:, :LANES] for p in yu_s)
     u_s = tuple(p[:, LANES:] for p in yu_s)
     w_s = tuple(p[:, LANES:] for p in xw_s)
-    send_ref[0, 0] = compact((eye + mm(y_s, give_s, TN)) * last)
-    send_ref[0, 1] = compact((mm(u_s, give_s, TN) + mm(values, key_s, TN)) * last)
-    send_ref[0, 2] = compact(mm(grads, query_s, TN) + mm(w_s, take_s, TN))
+    send_ref[at, 0] = compact((eye + mm(y_s, give_s, TN)) * last)
+    send_ref[at, 1] = compact((mm(u_s, give_s, TN) + mm(values, key_s, TN)) * last)
+    send_ref[at, 2] = compact(mm(grads, query_s, TN) + mm(w_s, take_s, TN))
+
+
+def lanes_of(refs, at):
+    return [ref.at[:, at * LANES : (at + 1) * LANES] for ref in refs]
+
+
+def local_kernel(*refs):
+    count = refs[0].shape[1] // LANES
+    firsts = [local_first(*lanes_of(refs[:7], at)) for at in range(count)]
+    inverses = invert([x for lowers, _ in firsts for x in lowers])
+    for at, (_, kept) in enumerate(firsts):
+        local_second(inverses[2 * at : 2 * at + 2], kept, at, *refs[7:])
 
 
 def scan_kernel(
@@ -334,18 +358,25 @@
     gd_ref[...] = (d_log * (-DECAY_SCALE) * sig * (1.0 - sig)).astype(BF16)
 
 
+def grads_kernel(*refs):
+    for at in range(refs[0].shape[1] // LANES):
+        one = [ref.at[at : at + 1] for ref in refs[7:9]]
+        grad_kernel(*lanes_of(refs[:7], at), *one, *lanes_of(refs[9:], at))
+
+
 def per_device(*arrays):
     rows, width = arrays[0].shape
     pairs = width // LANES
     n = lax.axis_size("ctx")
-    tokens = pl.BlockSpec((rows, LANES), lambda i: (0, i))
+    tokens = pl.BlockSpec((rows, LOCAL * LANES), lambda i: (0, i))
+    later = pl.BlockSpec((rows, LATER * LANES), lambda i: (0, i))
     wide = jax.ShapeDtypeStruct((rows, width), F32)
-    params = pltpu.CompilerParams(vmem_limit_bytes=48 * 1024 * 1024)
+    params = pltpu.CompilerParams(vmem_limit_bytes=60 * 1024 * 1024)
     local = pl.pallas_call(
         local_kernel,
-        grid=(pairs,),
+        grid=(pairs // LOCAL,),
         in_specs=[tokens] * 7,
-        out_specs=[pl.BlockSpec((1, 3, HS, LANES), lambda i: (i, 0, 0, 0))] + [tokens] * 6,
+        out_specs=[pl.BlockSpec((LOCAL, 3, HS, LANES), lambda i: (i, 0, 0, 0))] + [tokens] * 6,
         out_shape=[jax.ShapeDtypeStruct((pairs, 3, HS, LANES), F32)] + [wide] * 6,
         compiler_params=params,
     )(*arrays)
@@ -371,13 +402,13 @@
             collective_id=0, has_side_effects=True, vmem_limit_bytes=48 * 1024 * 1024
         ),
     )(local[0])
-    one = pl.BlockSpec((1, HS, LANES), lambda i: (i, 0, 0))
+    one = pl.BlockSpec((LATER, HS, LANES), lambda i: (i, 0, 0))
     return tuple(
         pl.pallas_call(
-            grad_kernel,
-            grid=(pairs,),
-            in_specs=[tokens] * 7 + [one, one] + [tokens] * 6,
-            out_specs=[tokens] * 6,
+            grads_kernel,
+            grid=(pairs // LATER,),
+            in_specs=[later] * 7 + [one, one] + [later] * 6,
+            out_specs=[later] * 6,
             out_shape=[jax.ShapeDtypeStruct((rows, width), BF16)] * 6,
             compiler_params=params,
         )(*arrays, start, end, *local[1:])

time: 171 us -> 137 us (0.80)
  Pallas kernels: 161 us -> 133 us
  local copies, waits for them, and re-layouts: 9.12 us -> 2.99 us
    pallas_call x2, Pallas kernels: 90.3 us -> 62.5 us  [the longest x1 34.4 us: per_device(): pl.pallas_call(local_kernel, grid=(pairs // LOCAL,), in_specs=[tokens] *...]
    unnamed x28 -> x6, local copies, waits for them, and re-layouts: 9.12 us -> 2.99 us
where the time goes in v2:
time: 137 us
  Pallas kernels  133 us (97%)
  local copies, waits for them, and re-layouts  2.99 us (2%)
    pallas_call x1, Pallas kernels, per_device(): pl.pallas_call(functools.partial(scan_kernel, n, pairs), in_specs=[vmem],...  70.7 us
    pallas_call x1, Pallas kernels, per_device(): pl.pallas_call(local_kernel, grid=(pairs // LOCAL,), in_specs=[tokens] *...  34.4 us
    pallas_call x1, Pallas kernels, per_device(): pl.pallas_call(grads_kernel, grid=(pairs // LATER,), in_specs=[later] * 7...  28.1 us
    unnamed x6, local copies, waits for them, and re-layouts  2.99 us

profile of v2, /device:TPU:0, one launch (start us, length us, event | category | flops | bytes accessed | tf_op | source)
XLA Modules:
  0.0 136.9 jit_solution(14051524609961436300)
XLA Ops:
  0.6 34.4 %shard_map.118 = (f32[16,3,64,128]{3,2,1,0:T(8,128)}, f32[128,2048]{1,0:T(8,128)}, f32[128,2048]{1,0:T(8,128)}, f32[128,2048]{1,0:T(8,128)}, f32[128,2048]{1,0:T...) custom-call(bf16[128,2048]{1,0:T(8,128)(2,1)} %refs_0_.3, bf16[128,2048]{1,0:T(8,128)(2,1)} %refs_1_.3, ...), custom_call_target="tpu_custom_call" | custom-call | tf_op jit(solution)/shard_map/pallas_call | solution.py:375
  35.0 0.0 copy-start
  35.0 1.4 %copy-done = f32[16,3,64,128]{3,2,1,0:T(8,128)S(1)} copy-done((f32[16,3,64,128]{3,2,1,0:T(8,128)S(1)}, f32[16,3,64,128]{3,2,1,0:T(8,128)}, u32[]{:S(2)}) %copy-start) | copy-done | bytes 1572888
  36.4 70.7 %shard_map.119 = (f32[16,64,128]{2,1,0:T(8,128)S(1)}, f32[16,64,128]{2,1,0:T(8,128)S(1)}) custom-call(f32[16,3,64,128]{3,2,1,0:T(8,128)S(1)} %copy-done), custom_call_target="tpu_custom_call" | custom-call | tf_op jit(solution)/shard_map/pallas_call | solution.py:385
  107.1 0.0 copy-start.1
  107.1 0.8 copy-done.1
  107.9 0.0 copy-start.2
  107.9 0.8 copy-done.2
  108.7 28.1 %shard_map.120 = (bf16[128,2048]{1,0:T(8,128)(2,1)}, bf16[128,2048]{1,0:T(8,128)(2,1)}, bf16[128,2048]{1,0:T(8,128)(2,1)}, bf16[128,2048]{1,0:T(8,128)(2,1)}, bf...) custom-call(bf16[128,2048]{1,0:T(8,128)(2,1)} %refs_0_.3, bf16[128,2048]{1,0:T(8,128)(2,1)} %refs_1_.3, ...), custom_call_target="tpu_custom_call" | custom-call | tf_op jit(solution)/shard_map/pallas_call | solution.py:407
Async XLA Ops:
  35.0 1.4 %copy-start = (f32[16,3,64,128]{3,2,1,0:T(8,128)S(1)}, f32[16,3,64,128]{3,2,1,0:T(8,128)}, u32[]{:S(2)}) copy-start(f32[16,3,64,128]{3,2,1,0:T(8,128)} %get-tuple-element.15.own_ref) | copy-start | bytes 4718596
  107.1 0.8 copy-start.1
  107.9 0.8 copy-start.2

commit v3 on v2

--- a/solution.py
+++ b/solution.py
@@ -236,7 +236,7 @@
         )
 
     def send(j, carry):
-        owner = lax.rem(me + j, pairs)
+        owner = lax.rem(me + pairs // 2 + j, pairs)
 
         @pl.when(owner != me)
         def _():

time: 137 us -> 132 us (0.964)
  Pallas kernels: 133 us -> 128 us
    pallas_call x1, Pallas kernels: 70.7 us -> 66 us  [per_device(): pl.pallas_call(functools.partial(scan_kernel, n, pairs), in_specs=[vmem],...]
where the time goes in v3:
time: 132 us
  Pallas kernels  128 us (97%)
  local copies, waits for them, and re-layouts  2.99 us (2%)
    pallas_call x1, Pallas kernels, per_device(): pl.pallas_call(functools.partial(scan_kernel, n, pairs), in_specs=[vmem],...  66 us
    pallas_call x1, Pallas kernels, per_device(): pl.pallas_call(local_kernel, grid=(pairs // LOCAL,), in_specs=[tokens] *...  34.4 us
    pallas_call x1, Pallas kernels, per_device(): pl.pallas_call(grads_kernel, grid=(pairs // LATER,), in_specs=[later] * 7...  28.1 us
    unnamed x6, local copies, waits for them, and re-layouts  2.99 us

profile of v3, /device:TPU:0, one launch (start us, length us, event | category | flops | bytes accessed | tf_op | source)
XLA Modules:
  0.0 132.3 jit_solution(6469046946843152273)
XLA Ops:
  0.6 34.4 %shard_map.118 = (f32[16,3,64,128]{3,2,1,0:T(8,128)}, f32[128,2048]{1,0:T(8,128)}, f32[128,2048]{1,0:T(8,128)}, f32[128,2048]{1,0:T(8,128)}, f32[128,2048]{1,0:T...) custom-call(bf16[128,2048]{1,0:T(8,128)(2,1)} %refs_0_.3, bf16[128,2048]{1,0:T(8,128)(2,1)} %refs_1_.3, ...), custom_call_target="tpu_custom_call" | custom-call | tf_op jit(solution)/shard_map/pallas_call | solution.py:375
  35.0 0.0 copy-start
  35.0 1.4 %copy-done = f32[16,3,64,128]{3,2,1,0:T(8,128)S(1)} copy-done((f32[16,3,64,128]{3,2,1,0:T(8,128)S(1)}, f32[16,3,64,128]{3,2,1,0:T(8,128)}, u32[]{:S(2)}) %copy-start) | copy-done | bytes 1572888
  36.4 66.0 %shard_map.119 = (f32[16,64,128]{2,1,0:T(8,128)S(1)}, f32[16,64,128]{2,1,0:T(8,128)S(1)}) custom-call(f32[16,3,64,128]{3,2,1,0:T(8,128)S(1)} %copy-done), custom_call_target="tpu_custom_call" | custom-call | tf_op jit(solution)/shard_map/pallas_call | solution.py:385
  102.4 0.0 copy-start.1
  102.4 0.8 copy-done.1
  103.2 0.0 copy-start.2
  103.2 0.8 copy-done.2
  104.0 28.1 %shard_map.120 = (bf16[128,2048]{1,0:T(8,128)(2,1)}, bf16[128,2048]{1,0:T(8,128)(2,1)}, bf16[128,2048]{1,0:T(8,128)(2,1)}, bf16[128,2048]{1,0:T(8,128)(2,1)}, bf...) custom-call(bf16[128,2048]{1,0:T(8,128)(2,1)} %refs_0_.3, bf16[128,2048]{1,0:T(8,128)(2,1)} %refs_1_.3, ...), custom_call_target="tpu_custom_call" | custom-call | tf_op jit(solution)/shard_map/pallas_call | solution.py:407
Async XLA Ops:
  35.0 1.4 %copy-start = (f32[16,3,64,128]{3,2,1,0:T(8,128)S(1)}, f32[16,3,64,128]{3,2,1,0:T(8,128)}, u32[]{:S(2)}) copy-start(f32[16,3,64,128]{3,2,1,0:T(8,128)} %get-tuple-element.15.own_ref) | copy-start | bytes 4718596
  102.4 0.8 copy-start.1
  103.2 0.8 copy-start.2
